TPU v7x, 512 devices: a whole 4x4x16 slice. The times are simulated.
512 devices in a mesh: blk: 8 (over x_lo, y), tm: 16 (over z), fsdp: 4 (over x_hi, core).
Axes of the slice: x: 4 (x_hi: 2, x_lo: 2; x = x_hi * 2 + x_lo), y: 4, z: 16, core: 2. Of those that a mesh axis runs over, the one named last changes fastest.
Arguments:
- features: bfloat16 [4, 16, 1280, 512], P('fsdp', 'tm', 'blk'), may hold values from -6 to 6
- neighbours: int32 [1280, 8], P('blk'), may hold values from 0 to 1279, as said below
- conv_taps: float32 [9, 512], replicated, may hold values from -3 to 3
- norm_gain: float32 [512], replicated, may hold values from 0.25 to 1.75
- qkv_weight: bfloat16 [512, 1536], P('fsdp'), as said below
- out_weight: bfloat16 [512, 512], P('fsdp'), may hold values from -0.25 to 0.25
- cotangent: bfloat16 [4, 16, 1280, 512], P('fsdp', 'tm', 'blk'), may hold values from -0.020874023 to 0.020874023
Outputs:
- weight_grads: float32 [1048576], P(('blk', 'tm', 'fsdp'))
Inputs may be any that keep to these rules, and one draw needn't show every extreme that they name: `neighbours`: row p holds p - 1, p + 1, three neighbouring pixels near p - 128 and three near p + 128, clipped to the window; every entry lies within 130 of p, and one lies exactly 130 away. `qkv_weight`: projection weights of order 512 ** -0.5 per entry.
All inputs are finite; a program needn't handle non-finite values.
Results may differ from a plain program's by a relative error of at most 0.0086.
Values may be sent and summed in bfloat16 or wider, within the bound.
A program may use at most 64 MiB of HBM per device.

v0:
```python
import jax
import jax.numpy as jnp
from jax import lax
from jax.sharding import PartitionSpec as P

HEADS = 8
HALO = 130


def with_halo(cells, sides, width):
    for axis, dim in sides:
        count = lax.axis_size(axis)
        ends = count - 1
        head = lax.slice_in_dim(cells, 0, width, axis=dim)
        tail = lax.slice_in_dim(cells, cells.shape[dim] - width, cells.shape[dim], axis=dim)
        cells = jnp.concatenate(
            [
                lax.ppermute(tail, axis, [(i, (i + 1) % count) for i in range(ends)]),
                cells,
                lax.ppermute(head, axis, [((i + 1) % count, i) for i in range(ends)]),
            ],
            axis=dim,
        )
    return cells


def rounded(values):
    return lax.optimization_barrier(values.astype(jnp.bfloat16)).astype(jnp.float32)


def attend_all(qkv_rows, grad_rows):
    frames, pixels, width = qkv_rows.shape
    channels = width // 3

    def split_heads(block):
        return block.reshape(frames, pixels, HEADS, channels // HEADS).astype(jnp.float32)

    queries = split_heads(qkv_rows[:, :, :channels])
    keys_all = split_heads(qkv_rows[:, :, channels : 2 * channels])
    values = split_heads(qkv_rows[:, :, 2 * channels :])
    grads = split_heads(grad_rows)
    scores = jnp.einsum("tpeh,upeh->petu", queries, keys_all) * 0.125
    causal = jnp.arange(frames)[:, None] >= jnp.arange(frames)[None, :]
    masked = jnp.where(causal, scores, -1e30)
    largest = jnp.max(masked, axis=-1, keepdims=True)
    totals = jnp.sum(jnp.exp(masked - largest), axis=-1, keepdims=True)
    log_total = largest + jnp.log(totals)
    weights = rounded(jnp.exp(masked - log_total))
    attended = jnp.einsum("petu,upeh->tpeh", weights, values)
    dprob = jnp.einsum("tpeh,upeh->petu", grads, values)
    delta = jnp.sum(weights * dprob, axis=-1, keepdims=True)
    dscore = rounded(weights * (dprob - delta) * 0.125)
    grad_query = jnp.einsum("petu,upeh->tpeh", dscore, keys_all)
    grad_key = jnp.einsum("petu,tpeh->upeh", dscore, queries)
    grad_value = jnp.einsum("petu,tpeh->upeh", weights, grads)
    joined = jnp.concatenate(
        [part.reshape(frames, pixels, channels) for part in (grad_query, grad_key, grad_value)],
        axis=-1,
    )
    return (
        attended.reshape(frames, pixels, channels).astype(jnp.bfloat16),
        joined.astype(jnp.bfloat16),
    )


def per_device(features, neighbours, conv_taps, norm_gain, qkv_weight, out_weight, cotangent):
    inputs = features[0, 0]
    upstream = cotangent[0, 0]
    pixels, channels = inputs.shape
    padded = with_halo(inputs, (("blk", 0),), HALO)
    first_pixel = lax.axis_index("blk") * pixels
    local_rows = neighbours - first_pixel + HALO
    inputs_f = inputs.astype(jnp.float32)
    spatial = conv_taps[0] * inputs_f
    for column in range(8):
        spatial = spatial + conv_taps[column + 1] * jnp.take(
            padded, local_rows[:, column], axis=0
        ).astype(jnp.float32)
    hidden_f = rounded(inputs_f + spatial)
    inverse = lax.rsqrt(jnp.mean(hidden_f * hidden_f, axis=-1, keepdims=True) + 1e-05)
    normed = (hidden_f * inverse * norm_gain).astype(jnp.bfloat16)
    full_qkv, full_out = (
        lax.all_gather(qkv_weight, "fsdp", axis=0, tiled=True),
        lax.all_gather(out_weight, "fsdp", axis=0, tiled=True),
    )
    att_grads = jnp.dot(upstream, full_out.T, preferred_element_type=jnp.float32).astype(
        jnp.bfloat16
    )
    swap_normed, swap_grads, swap_upstream = (
        lax.all_to_all(normed[None], "tm", split_axis=1, concat_axis=0, tiled=True),
        lax.all_to_all(att_grads[None], "tm", split_axis=1, concat_axis=0, tiled=True),
        lax.all_to_all(upstream[None], "tm", split_axis=1, concat_axis=0, tiled=True),
    )
    frames = swap_normed.shape[0]
    few_pixels = swap_normed.shape[1]
    flat_normed = swap_normed.reshape(-1, channels)
    qkv_rows = jnp.dot(flat_normed, full_qkv, preferred_element_type=jnp.float32).astype(
        jnp.bfloat16
    )
    qkv_rows = qkv_rows.reshape(frames, few_pixels, 3 * channels)
    attended_x, dqkv_x = attend_all(qkv_rows, swap_grads)
    grad_in = jnp.einsum(
        "pc,pd->cd",
        flat_normed,
        dqkv_x.reshape(-1, 3 * channels),
        preferred_element_type=jnp.float32,
    )
    grad_out = jnp.einsum(
        "pc,pd->cd",
        attended_x.reshape(-1, channels),
        swap_upstream.reshape(-1, channels),
        preferred_element_type=jnp.float32,
    )
    summands = jnp.concatenate([grad_in.reshape(-1), grad_out.reshape(-1)])
    return lax.psum_scatter(summands, ("blk", "tm", "fsdp"), scatter_dimension=0, tiled=True)


def solution(mesh):
    return jax.shard_map(
        per_device,
        mesh=mesh,
        in_specs=(
            P("fsdp", "tm", "blk", None),
            P("blk", None),
            P(),
            P(),
            P("fsdp", None),
            P("fsdp", None),
            P("fsdp", "tm", "blk", None),
        ),
        out_specs=P(("blk", "tm", "fsdp")),
        check_vma=False,
    )
```

profile of v0, /device:TPU:1, one launch (start us, length us, event | category | flops | bytes accessed | tf_op | source)
XLA Modules:
  0.0 608.1 jit_solution(18186007467948523333)
XLA Ops:
  6.6 1.1 slice_bitcast_fusion.1
  7.6 4.0 collective-permute-start
  11.7 1.3 collective-permute-start.1
  13.0 12.2 %all_gather.7 = bf16[512,512]{1,0:T(8,128)(2,1)S(1)} all-gather(bf16[128,512]{1,0:T(8,128)(2,1)} %param.14), channel_id=1, replica_groups=mesh['blk'=8,'tm'=16,'fsdp'=4] {'fsdp'}, dimensions={0}, use_global_device_ids=true | all-gather | bytes 655360 | tf_op jit(solution)/shard_map/all_gather | solution.py:84
  25.2 1.2 fusion.10
  26.4 0.3 copy.113
  26.7 0.5 broadcast.56
  27.2 1.6 reduce.4
  28.8 0.7 reshape.187
  29.6 12.4 %all-to-all-start.1 = ((bf16[16,2,2560]{2,1,0:T(2,128)(2,1)}), bf16[16,2,2560]{2,1,0:T(2,128)(2,1)S(1)}, u32[]{:S(2)}, u32[]{:S(2)}) async-start(bf16[16,2,2560]{2,1,0:T(2,128)(2,1)} %reshape.187), calls=%async_computation.1 | async-start | bytes 327680 | tf_op jit(solution)/shard_map/all_to_all | solution.py:91
  42.3 0.3 copy.112
  42.6 1.6 reduce.3
  44.2 0.7 reshape.185
  45.1 0.9 gather_fusion.2
  46.0 0.9 gather_fusion.3
  46.9 0.9 gather_fusion.4
  47.9 0.9 gather_fusion.5
  48.8 0.9 gather_fusion.6
  49.7 0.9 gather_fusion.7
  50.7 0.9 gather_fusion
  51.6 0.9 gather_fusion.1
  52.5 2.2 all-to-all-done.1
  54.7 9.3 %all-to-all-start.2 = ((bf16[16,2,2560]{2,1,0:T(2,128)(2,1)}), bf16[16,2,2560]{2,1,0:T(2,128)(2,1)S(1)}, u32[]{:S(2)}, u32[]{:S(2)}) async-start(bf16[16,2,2560]{2,1,0:T(2,128)(2,1)} %reshape.185), calls=%async_computation.2 | async-start | bytes 327680 | tf_op jit(solution)/shard_map/all_to_all | solution.py:92
  64.0 0.5 fusion.26
  64.5 0.1 fusion.27
  64.7 0.1 fusion.39
  64.8 0.3 copy.114
  65.1 1.6 reduce.2
  66.7 0.7 reshape.183
  67.4 8.8 %all-to-all-done.2 = bf16[16,2,2560]{2,1,0:T(2,128)(2,1)S(1)} async-done(((bf16[16,2,2560]{2,1,0:T(2,128)(2,1)}), bf16[16,2,2560]{2,1,0:T(2,128)(2,1)S(1)}, u32[]{:S(2)}, u32[]{:S(2)}) %all-to-all-start.2) | async-done | bytes 163872 | tf_op jit(solution)/shard_map/all_to_all | solution.py:92
  76.2 7.5 %all-to-all-start = ((bf16[16,2,2560]{2,1,0:T(2,128)(2,1)}), bf16[16,2,2560]{2,1,0:T(2,128)(2,1)S(1)}, u32[]{:S(2)}, u32[]{:S(2)}) async-start(bf16[16,2,2560]{2,1,0:T(2,128)(2,1)} %reshape.183), calls=%async_computation | async-start | bytes 327680 | tf_op jit(solution)/shard_map/all_to_all | solution.py:90
  83.8 0.2 all-reduce.3.cloned.1.call-start
  84.0 0.1 reshape.188
  84.1 0.9 bitcast_reduce_fusion
  85.1 0.2 reshape.86
  85.3 0.9 reshape.186
  86.1 9.8 %all-to-all-done = bf16[16,2,2560]{2,1,0:T(2,128)(2,1)S(1)} async-done(((bf16[16,2,2560]{2,1,0:T(2,128)(2,1)}), bf16[16,2,2560]{2,1,0:T(2,128)(2,1)S(1)}, u32[]{:S(2)}, u32[]{:S(2)}) %all-to-all-start) | async-done | bytes 163872 | tf_op jit(solution)/shard_map/all_to_all | solution.py:90
  96.0 0.1 reshape.184
  96.1 1.8 convolution_convert_fusion
  98.0 0.2 reshape.83
  98.2 0.2 reshape.181
  98.5 0.2 reshape.179
  98.7 0.2 reshape.180
  98.9 0.3 fusion.51
  99.3 0.2 exponential_reduce_fusion
  99.5 0.1 exponential_convert_fusion
  99.6 0.3 fusion.31
  99.9 0.2 fusion.5
  100.2 0.3 fusion.6
  100.5 0.3 fusion.8
  100.8 0.3 fusion.9
  101.1 1.0 fusion.7
  102.2 0.2 concatenate.18
  102.5 0.2 concatenate.19
  102.9 0.2 concatenate.20
  103.1 2.3 fusion.12
  105.4 2.7 reshape.88
  108.0 1.1 copy.64
  109.1 0.9 convert_element_type.87
  110.0 1.4 convolution_bitcast_fusion
  111.4 0.3 copy.76
  111.7 2.2 pad_maximum_fusion
  113.9 486.1 %all-reduce.3.cloned.1.call-done = f32[1048576]{0:T(1024)} async-done(((f32[1048576]{0:T(1024)}), f32[1048576]{0:T(1024)}) %all-reduce.3.cloned.1.call-update) | async-done | bytes 4194320
  600.0 1.3 dynamic-slice
  (47 shorter events, 0.7 us)
Async XLA Ops:
  6.5 38.4 %copy-start = (bf16[1,1,160,512]{3,2,1,0:T(8,128)(2,1)S(1)}, bf16[1,1,160,512]{3,2,1,0:T(8,128)(2,1)}, u32[]{:S(2)}) copy-start(bf16[1,1,160,512]{3,2,1,0:T(8,128)(2,1)} %param.9) | copy-start | bytes 491524
  6.5 35.8 %copy-start.1 = (bf16[1,1,160,512]{3,2,1,0:T(8,128)(2,1)S(1)}, bf16[1,1,160,512]{3,2,1,0:T(8,128)(2,1)}, u32[]{:S(2)}) copy-start(bf16[1,1,160,512]{3,2,1,0:T(8,128)(2,1)} %param.15) | copy-start | bytes 491524
  6.5 35.5 %copy-start.3 = (s32[160,8]{0,1:T(8,128)S(1)}, s32[160,8]{0,1:T(8,128)}, u32[]{:S(2)}) copy-start(s32[160,8]{0,1:T(8,128)} %param.10) | copy-start | bytes 15364
  6.5 35.7 %copy-start.2 = (f32[9,512]{1,0:T(8,128)S(1)}, f32[9,512]{1,0:T(8,128)}, u32[]{:S(2)}) copy-start(f32[9,512]{1,0:T(8,128)} %param.11) | copy-start | bytes 55300
  6.5 89.6 %all-gather.2.cloned.1.call-start = ((), (), s32[]{:S(2)}) async-start(), calls=%async_computation.3 | async-start | bytes 1966080 | tf_op jit(solution)/shard_map/all_gather | solution.py:83
  7.6 37.3 %collective-permute-start = (bf16[130,512]{1,0:T(8,128)(2,1)S(1)}, bf16[130,512]{1,0:T(8,128)(2,1)S(1)}, u32[]{:S(2)}, u32[]{:S(2)}) collective-permute-start(bf16[130,512]{1,0:T(8,128)(2,1)S(1)} %get-tuple-element.9), channel_id=1, source_target_pairs={{0,64},{64,128},{128,192},{192,256},{256,320},{320,384},{384,448},... | collective-permute-start | bytes 399368 | tf_op jit(solution)/shard_map/ppermute | solution.py:18
  11.7 33.3 %collective-permute-start.1 = (bf16[130,512]{1,0:T(8,128)(2,1)S(1)}, bf16[130,512]{1,0:T(8,128)(2,1)S(1)}, u32[]{:S(2)}, u32[]{:S(2)}) collective-permute-start(bf16[130,512]{1,0:T(8,128)(2,1)S(1)} %get-tuple-element.10), channel_id=1, source_target_pairs={{64,0},{128,64},{192,128},{256,192},{320,256},{384,320},{448,384},... | collective-permute-start | bytes 399368 | tf_op jit(solution)/shard_map/ppermute | solution.py:20
  29.6 25.1 %all-to-all-start.1 = ((bf16[16,2,2560]{2,1,0:T(2,128)(2,1)}), bf16[16,2,2560]{2,1,0:T(2,128)(2,1)S(1)}, u32[]{:S(2)}, u32[]{:S(2)}) async-start(bf16[16,2,2560]{2,1,0:T(2,128)(2,1)} %reshape.187), calls=%async_computation.1 | async-start | bytes 327680 | tf_op jit(solution)/shard_map/all_to_all | solution.py:91
  49.7 14.9 %copy-start.4 = (f32[512]{0:T(512)S(1)}, f32[512]{0:T(512)}, u32[]{:S(2)}) copy-start(f32[512]{0:T(512)} %param.12) | copy-start | bytes 6148
  54.7 21.5 %all-to-all-start.2 = ((bf16[16,2,2560]{2,1,0:T(2,128)(2,1)}), bf16[16,2,2560]{2,1,0:T(2,128)(2,1)S(1)}, u32[]{:S(2)}, u32[]{:S(2)}) async-start(bf16[16,2,2560]{2,1,0:T(2,128)(2,1)} %reshape.185), calls=%async_computation.2 | async-start | bytes 327680 | tf_op jit(solution)/shard_map/all_to_all | solution.py:92
  76.2 19.7 %all-to-all-start = ((bf16[16,2,2560]{2,1,0:T(2,128)(2,1)}), bf16[16,2,2560]{2,1,0:T(2,128)(2,1)S(1)}, u32[]{:S(2)}, u32[]{:S(2)}) async-start(bf16[16,2,2560]{2,1,0:T(2,128)(2,1)} %reshape.183), calls=%async_computation | async-start | bytes 327680 | tf_op jit(solution)/shard_map/all_to_all | solution.py:90
  83.8 516.2 %all-reduce.3.cloned.1.call-start = ((), (), s32[]{:S(2)}) async-start(), calls=%async_computation.4 | async-start | bytes 8388608
Sparse Core Ops, SparseCore 0:
  13.1 37.5 all-gather.1
  114.0 485.9 all-reduce.2
where the time goes:
time: 610 us; the launch traced here: 608 us
  waiting for transfers between devices  507 us (83%)
  starting transfers between devices  34.8 us (6%)
  local copies, waits for them, and re-layouts  22.3 us (4%)
  between operations  14 us (2%)
  blocking collectives  12.2 us (2%)
  matrix products  9.32 us (2%)
  other arithmetic  8.56 us (1%)
    unnamed x3, waiting for transfers between devices  486 us
    all_to_all x1, starting transfers between devices, per_device(): lax.all_to_all(att_grads[None], 'tm', split_axis=1, concat_axis=0, tiled=...  12.4 us
    all_gather x1, blocking collectives, per_device(): lax.all_gather(out_weight, 'fsdp', axis=0, tiled=True)  12.2 us
  transfers between devices with their start and end apart: 7, of which 4 were waited for; matrix products, arithmetic and copies ran while one was open for 3% of the time, Pallas kernels for 0%

commit v1 on v0

--- a/solution.py
+++ b/solution.py
@@ -1,10 +1,182 @@
+import functools
+
 import jax
 import jax.numpy as jnp
 from jax import lax
+from jax.experimental import pallas as pl
+from jax.experimental.pallas import tpu as pltpu
 from jax.sharding import PartitionSpec as P
 
 HEADS = 8
 HALO = 130
+MESH = pl.DeviceIdType.MESH
+F32 = jnp.float32
+BF16 = jnp.bfloat16
+
+
+def reduce_kernel(
+    part,
+    out,
+    core_out,
+    core_in,
+    xs_out,
+    xs_in,
+    ys_out,
+    ys_in,
+    xs_sum,
+    ys_sum,
+    xs_out2,
+    xs_in2,
+    ys_out2,
+    ys_in2,
+    z_sum,
+    z_out,
+    z_in,
+    core_sems,
+    one_sems,
+    two_sems,
+    z_sems,
+):
+    blk = lax.axis_index("blk")
+    zed = lax.axis_index("tm")
+    fsdp = lax.axis_index("fsdp")
+    x_lo, y = blk // 4, blk % 4
+    x_hi, core = fsdp // 2, fsdp % 2
+    x = x_hi * 2 + x_lo
+
+    def at_x(to):
+        return ((to % 2) * 4 + y, zed, (to // 2) * 2 + core)
+
+    def at_y(to):
+        return (x_lo * 4 + to, zed, fsdp)
+
+    def at_z(to):
+        return (blk, to, fsdp)
+
+    mate = (blk, zed, x_hi * 2 + 1 - core)
+    partners = [mate]
+    partners += [at_x((x + d) % 4) for d in (1, 2, 3)]
+    partners += [at_y((y + d) % 4) for d in (1, 2, 3)]
+    partners += [at_z((zed + d) % 16) for d in range(1, 16)]
+    barrier = pltpu.get_barrier_semaphore()
+    for partner in partners:
+        pl.semaphore_signal(barrier, inc=1, device_id=partner, device_id_type=MESH)
+
+    for hi in range(2):
+        for lo in range(2):
+            for j in range(4):
+                core_out[hi * 2 + lo, j] = part[lo, j, :, hi, 1 - core].astype(BF16)
+    pl.semaphore_wait(barrier, len(partners))
+
+    def send(src, dst, sems, slot, to):
+        copy = pltpu.make_async_remote_copy(
+            src_ref=src,
+            dst_ref=dst,
+            send_sem=sems.at[0, slot],
+            recv_sem=sems.at[1, slot],
+            device_id=to,
+            device_id_type=MESH,
+        )
+        copy.start()
+        return copy
+
+    first = send(core_out, core_in, core_sems, 0, mate)
+    first.wait()
+
+    def chip(hi, lo, j):
+        return part[lo, j, :, hi, core] + core_in[hi * 2 + lo, j].astype(F32)
+
+    for hi in range(2):
+        for lo in range(2):
+            for j in range(4):
+                total = chip(hi, lo, j)
+                xs_out[hi * 2 + lo, j] = total[:8].astype(BF16)
+                ys_out[j, hi * 2 + lo] = total[8:].astype(BF16)
+    ones = []
+    for d in (2, 1, 3):
+        to = (x + d) % 4
+        ones.append(send(xs_out.at[to], xs_in.at[d - 1], one_sems, d - 1, at_x(to)))
+        to = (y + d) % 4
+        ones.append(send(ys_out.at[to], ys_in.at[d - 1], one_sems, d + 2, at_y(to)))
+    for j in range(4):
+        xs_sum[j] = part[x_lo, j, 0:8, x_hi, core] + core_in[x, j, 0:8].astype(F32)
+        ys_sum[j] = part[j % 2, y, 8:16, j // 2, core] + core_in[j, y, 8:16].astype(F32)
+    for copy in ones:
+        copy.wait_recv()
+    for j in range(4):
+        total = xs_sum[j]
+        for d in range(3):
+            total += xs_in[d, j].astype(F32)
+        xs_sum[j] = total
+        xs_out2[j] = total.astype(BF16)
+        total = ys_sum[j]
+        for d in range(3):
+            total += ys_in[d, j].astype(F32)
+        ys_sum[j] = total
+        ys_out2[j] = total.astype(BF16)
+    twos = []
+    for d in (2, 1, 3):
+        to = (y + d) % 4
+        twos.append(send(xs_out2.at[to], xs_in2.at[d - 1], two_sems, d - 1, at_y(to)))
+        to = (x + d) % 4
+        twos.append(send(ys_out2.at[to], ys_in2.at[d - 1], two_sems, d + 2, at_x(to)))
+    for copy in twos:
+        copy.wait_recv()
+    low, high = xs_sum[y], ys_sum[x]
+    for d in range(3):
+        low += xs_in2[d].astype(F32)
+        high += ys_in2[d].astype(F32)
+    z_sum[0:8] = low
+    z_sum[8:16] = high
+    z_out[0:8] = low.astype(BF16)
+    z_out[8:16] = high.astype(BF16)
+    threes = []
+    for d in (8, 7, 9, 6, 10, 5, 11, 4, 12, 3, 13, 2, 14, 1, 15):
+        to = (zed + d) % 16
+        threes.append(send(z_out.at[to], z_in.at[d - 1], z_sems, d - 1, at_z(to)))
+    for copy in threes:
+        copy.wait_recv()
+    total = z_sum[zed]
+    for d in range(15):
+        total += z_in[d].astype(F32)
+    out[...] = total
+    for copy in ones + twos + threes:
+        copy.wait_send()
+
+
+def reduce_scatter(summands):
+    part = summands.reshape(2, 4, 16, 2, 2, 16, 128)
+    tile = (16, 128)
+    return pl.pallas_call(
+        reduce_kernel,
+        out_shape=jax.ShapeDtypeStruct(tile, F32),
+        in_specs=[pl.BlockSpec(memory_space=pltpu.VMEM)],
+        out_specs=pl.BlockSpec(memory_space=pltpu.VMEM),
+        scratch_shapes=[
+            pltpu.VMEM((4, 4, 16) + tile, BF16),
+            pltpu.VMEM((4, 4, 16) + tile, BF16),
+            pltpu.VMEM((4, 4, 8) + tile, BF16),
+            pltpu.VMEM((3, 4, 8) + tile, BF16),
+            pltpu.VMEM((4, 4, 8) + tile, BF16),
+            pltpu.VMEM((3, 4, 8) + tile, BF16),
+            pltpu.VMEM((4, 8) + tile, F32),
+            pltpu.VMEM((4, 8) + tile, F32),
+            pltpu.VMEM((4, 8) + tile, BF16),
+            pltpu.VMEM((3, 8) + tile, BF16),
+            pltpu.VMEM((4, 8) + tile, BF16),
+            pltpu.VMEM((3, 8) + tile, BF16),
+            pltpu.VMEM((16,) + tile, F32),
+            pltpu.VMEM((16,) + tile, BF16),
+            pltpu.VMEM((15,) + tile, BF16),
+            pltpu.SemaphoreType.DMA((2, 1)),
+            pltpu.SemaphoreType.DMA((2, 6)),
+            pltpu.SemaphoreType.DMA((2, 6)),
+            pltpu.SemaphoreType.DMA((2, 15)),
+        ],
+        compiler_params=pltpu.CompilerParams(
+            collective_id=0, has_side_effects=True, vmem_limit_bytes=48 * 1024 * 1024
+        ),
+    )(part).reshape(-1)
 
 
 def with_halo(cells, sides, width):
@@ -112,7 +284,7 @@
         preferred_element_type=jnp.float32,
     )
     summands = jnp.concatenate([grad_in.reshape(-1), grad_out.reshape(-1)])
-    return lax.psum_scatter(summands, ("blk", "tm", "fsdp"), scatter_dimension=0, tiled=True)
+    return reduce_scatter(summands)
 
 
 def solution(mesh):

time: 610 us -> 160 us (0.26)
  waiting for transfers between devices: 507 us -> 20.9 us
  Pallas kernels: 0 us -> 33.9 us
    unnamed x3 -> x1, waiting for transfers between devices: 486 us -> 0.71 us
    pallas_call x0 -> x1, Pallas kernels: none -> 33.9 us  [reduce_scatter(): pl.pallas_call(reduce_kernel, out_shape=jax.ShapeDtypeStruct(tile, F32),...]
    all_to_all x1, waiting for transfers between devices: 8.83 us -> 0.01 us  [per_device(): lax.all_to_all(upstream[None], 'tm', split_axis=1, concat_axis=0, tiled=T...]
    all_to_all x1, waiting for transfers between devices: 2.16 us -> 9.32 us  [per_device(): lax.all_to_all(att_grads[None], 'tm', split_axis=1, concat_axis=0, tiled=...]
  transfers between devices with their start and end apart: 7 -> 6, of which waited for: 4 -> 2; matrix products, arithmetic and copies ran while one was open for 3% -> 13% of each run, Pallas kernels for 0% -> 0%
where the time goes in v1:
time: 160 us; the launch traced here: 159 us
  starting transfers between devices  39.3 us (25%)
  Pallas kernels  33.9 us (21%)
  local copies, waits for them, and re-layouts  22.3 us (14%)
  waiting for transfers between devices  20.9 us (13%)
  between operations  13.9 us (9%)
  blocking collectives  13.2 us (8%)
  other arithmetic  9.53 us (6%)
  matrix products  5.87 us (4%)
    pallas_call x1, Pallas kernels, reduce_scatter(): pl.pallas_call(reduce_kernel, out_shape=jax.ShapeDtypeStruct(tile, F32),...  33.9 us
    all_to_all x1, starting transfers between devices, per_device(): lax.all_to_all(upstream[None], 'tm', split_axis=1, concat_axis=0, tiled=T...  14.9 us
    all_gather x1, blocking collectives, per_device(): lax.all_gather(out_weight, 'fsdp', axis=0, tiled=True)  13.2 us
    all_to_all x1, starting transfers between devices, per_device(): lax.all_to_all(att_grads[None], 'tm', split_axis=1, concat_axis=0, tiled=...  11.8 us
    all_to_all x1, waiting for transfers between devices, per_device(): lax.all_to_all(normed[None], 'tm', split_axis=1, concat_axis=0, tiled=True)  10.8 us
    all_to_all x1, waiting for transfers between devices, per_device(): lax.all_to_all(att_grads[None], 'tm', split_axis=1, concat_axis=0, tiled=...  9.32 us
    gather x8, local copies, waits for them, and re-layouts, per_device(): jnp.take(padded, local_rows[:, column], axis=0).astype(jnp.float32)  7.45 us
    all_to_all x1, starting transfers between devices, per_device(): lax.all_to_all(normed[None], 'tm', split_axis=1, concat_axis=0, tiled=True)  7.31 us
  transfers between devices with their start and end apart: 6, of which 2 were waited for; matrix products, arithmetic and copies ran while one was open for 13% of the time, Pallas kernels for 0%

profile of v1, /device:TPU:1, one launch (start us, length us, event | category | flops | bytes accessed | tf_op | source)
XLA Modules:
  0.0 158.9 jit_solution(13919018031305577518)
XLA Ops:
  6.5 0.7 all-gather.2.cloned.1.call-update
  7.3 1.0 slice_bitcast_fusion.1
  8.3 4.0 %collective-permute-start = (bf16[130,512]{1,0:T(8,128)(2,1)S(1)}, bf16[130,512]{1,0:T(8,128)(2,1)S(1)}, u32[]{:S(2)}, u32[]{:S(2)}) collective-permute-start(bf16[130,512]{1,0:T(8,128)(2,1)S(1)} %get-tuple-element.9), channel_id=1, source_target_pairs={{0,64},{64,128},{128,192},{192,256},{256,320},{320,384},{384,448},... | collective-permute-start | bytes 399368 | tf_op jit(solution)/shard_map/ppermute | solution.py:190
  12.3 1.3 collective-permute-start.1
  13.6 1.2 copy.112
  14.8 0.5 broadcast.56
  15.3 1.6 %reduce.3 = bf16[160,512]{1,0:T(8,128)(2,1)S(1)} reduce(bf16[160,1,512]{2,1,0:T(2,128)(2,1)S(1)} %bitcast.84, bf16[]{:T(256)} %broadcast.56), dimensions={1}, to_apply=%bitcast.77.reduce_sub_computation | reduce | bytes 327682
  16.9 0.7 reshape.193
  17.7 14.9 %all-to-all-start.2 = ((bf16[16,2,2560]{2,1,0:T(2,128)(2,1)}), bf16[16,2,2560]{2,1,0:T(2,128)(2,1)S(1)}, u32[]{:S(2)}, u32[]{:S(2)}) async-start(bf16[16,2,2560]{2,1,0:T(2,128)(2,1)} %reshape.193), calls=%async_computation.2 | async-start | bytes 327680 | tf_op jit(solution)/shard_map/all_to_all | solution.py:264
  32.6 0.7 subtract_add_fusion
  33.5 13.2 %all_gather.7 = bf16[512,512]{1,0:T(8,128)(2,1)S(1)} all-gather(bf16[128,512]{1,0:T(8,128)(2,1)} %param.14), channel_id=1, replica_groups=mesh['blk'=8,'tm'=16,'fsdp'=4] {'fsdp'}, dimensions={0}, use_global_device_ids=true | all-gather | bytes 655360 | tf_op jit(solution)/shard_map/all_gather | solution.py:256
  46.7 0.3 fusion.10
  47.1 0.3 copy.113
  47.4 1.6 %reduce.4 = bf16[160,512]{1,0:T(8,128)(2,1)S(1)} reduce(bf16[160,1,512]{2,1,0:T(2,128)(2,1)S(1)} %bitcast.86, bf16[]{:T(256)} %broadcast.56), dimensions={1}, to_apply=%bitcast.78.reduce_sub_computation | reduce | bytes 327682
  49.0 0.8 reshape.195
  49.9 0.9 gather_fusion.7
  50.8 0.9 gather_fusion.6
  51.8 0.9 gather_fusion.5
  52.7 0.9 gather_fusion.4
  53.6 0.9 gather_fusion.3
  54.6 0.9 gather_fusion.2
  55.5 0.9 gather_fusion.1
  56.4 0.9 gather_fusion
  57.4 11.8 %all-to-all-start.1 = ((bf16[16,2,2560]{2,1,0:T(2,128)(2,1)}), bf16[16,2,2560]{2,1,0:T(2,128)(2,1)S(1)}, u32[]{:S(2)}, u32[]{:S(2)}) async-start(bf16[16,2,2560]{2,1,0:T(2,128)(2,1)} %reshape.195), calls=%async_computation.1 | async-start | bytes 327680 | tf_op jit(solution)/shard_map/all_to_all | solution.py:263
  69.1 0.5 fusion.26
  69.6 0.1 fusion.27
  69.8 0.1 fusion.39
  69.9 0.3 copy.114
  70.2 1.6 %reduce.2 = bf16[160,512]{1,0:T(8,128)(2,1)S(1)} reduce(bf16[160,1,512]{2,1,0:T(2,128)(2,1)S(1)} %bitcast.85, bf16[]{:T(256)} %broadcast.56), dimensions={1}, to_apply=%bitcast.79.reduce_sub_computation | reduce | bytes 327682
  71.8 0.7 reshape.191
  72.5 9.3 %all-to-all-done.1 = bf16[16,2,2560]{2,1,0:T(2,128)(2,1)S(1)} async-done(((bf16[16,2,2560]{2,1,0:T(2,128)(2,1)}), bf16[16,2,2560]{2,1,0:T(2,128)(2,1)S(1)}, u32[]{:S(2)}, u32[]{:S(2)}) %all-to-all-start.1) | async-done | bytes 163872 | tf_op jit(solution)/shard_map/all_to_all | solution.py:263
  81.8 7.3 %all-to-all-start = ((bf16[16,2,2560]{2,1,0:T(2,128)(2,1)}), bf16[16,2,2560]{2,1,0:T(2,128)(2,1)S(1)}, u32[]{:S(2)}, u32[]{:S(2)}) async-start(bf16[16,2,2560]{2,1,0:T(2,128)(2,1)} %reshape.191), calls=%async_computation | async-start | bytes 327680 | tf_op jit(solution)/shard_map/all_to_all | solution.py:262
  89.2 0.1 reshape.196
  89.3 0.9 bitcast_reduce_fusion
  90.2 0.2 reshape.92
  90.4 0.1 reshape.194
  90.5 10.8 %all-to-all-done = bf16[16,2,2560]{2,1,0:T(2,128)(2,1)S(1)} async-done(((bf16[16,2,2560]{2,1,0:T(2,128)(2,1)}), bf16[16,2,2560]{2,1,0:T(2,128)(2,1)S(1)}, u32[]{:S(2)}, u32[]{:S(2)}) %all-to-all-start) | async-done | bytes 163872 | tf_op jit(solution)/shard_map/all_to_all | solution.py:262
  101.4 0.1 reshape.192
  101.5 1.8 %convolution_convert_fusion = bf16[160,1536]{1,0:T(8,128)(2,1)S(1)} fusion(bf16[512,1536]{1,0:T(8,128)(2,1)} %all-gather.2.cloned.1.call-done, bf16[1,160,512]{2,0,1:T(2,128)(2,1)S(1)} %bitcast.87), kind=kOutput, calls=%fused_computation.10 | convolution fusion | flops 251904000 | bytes 2228224 | tf_op jit(solution)/shard_map/dot_general | solution.py:269
  103.4 0.2 reshape.89
  103.6 0.2 reshape.189
  103.9 0.2 reshape.188
  104.1 0.2 reshape.187
  104.3 0.3 fusion.51
  104.6 0.2 exponential_reduce_fusion
  104.9 0.1 exponential_convert_fusion
  105.0 0.3 fusion.31
  105.3 0.2 fusion.5
  105.6 0.3 fusion.8
  105.9 0.3 fusion.6
  106.2 0.3 fusion.7
  106.5 0.3 fusion.9
  106.8 0.1 copy.57
  106.9 0.9 concatenate.18
  107.9 0.9 concatenate.19
  108.9 0.9 concatenate.20
  109.8 0.2 convert_element_type.87
  110.1 0.3 convolution_bitcast_fusion
  110.4 1.2 copy.76
  111.7 1.5 fusion.12
  113.2 1.9 %reshape.94 = f32[786432]{0:T(1024)} reshape(f32[512,1536]{1,0:T(8,128)S(1)} %fusion.12) | data formatting | bytes 6291456 | tf_op jit(solution)/shard_map/reshape | solution.py:286
  115.1 2.5 %pad_maximum_fusion = f32[1048576]{0:T(1024)S(1)} fusion(f32[262144]{0:T(1024)} %bitcast.82, f32[786432]{0:T(1024)} %reshape.94), kind=kLoop, calls=%fused_computation.9 | loop fusion | flops 1048576 | bytes 8388608 | tf_op jit(solution)/shard_map/concatenate | solution.py:286
  117.6 33.9 %shard_map.73 = f32[16,128]{1,0:T(8,128)S(1)} custom-call(f32[2,4,16,2,2,16,128]{6,5,4,3,2,1,0:T(8,128)S(1)} %bitcast.80), custom_call_target="tpu_custom_call" | custom-call | tf_op jit(solution)/shard_map/pallas_call | solution.py:150
  151.5 0.6 copy.116
  (47 shorter events, 0.6 us)
Async XLA Ops:
  6.5 43.3 %copy-start = (bf16[1,1,160,512]{3,2,1,0:T(8,128)(2,1)S(1)}, bf16[1,1,160,512]{3,2,1,0:T(8,128)(2,1)}, u32[]{:S(2)}) copy-start(bf16[1,1,160,512]{3,2,1,0:T(8,128)(2,1)} %param.9) | copy-start | bytes 491524
  6.5 40.2 %copy-start.1 = (bf16[1,1,160,512]{3,2,1,0:T(8,128)(2,1)S(1)}, bf16[1,1,160,512]{3,2,1,0:T(8,128)(2,1)}, u32[]{:S(2)}) copy-start(bf16[1,1,160,512]{3,2,1,0:T(8,128)(2,1)} %param.15) | copy-start | bytes 491524
  6.5 40.6 %copy-start.4 = (f32[9,512]{1,0:T(8,128)S(1)}, f32[9,512]{1,0:T(8,128)}, u32[]{:S(2)}) copy-start(f32[9,512]{1,0:T(8,128)} %param.11) | copy-start | bytes 55300
  6.5 95.0 %all-gather.2.cloned.1.call-start = ((), (), s32[]{:S(2)}) async-start(), calls=%async_computation.3 | async-start | bytes 1966080 | tf_op jit(solution)/shard_map/all_gather | solution.py:255
  8.3 41.5 %collective-permute-start = (bf16[130,512]{1,0:T(8,128)(2,1)S(1)}, bf16[130,512]{1,0:T(8,128)(2,1)S(1)}, u32[]{:S(2)}, u32[]{:S(2)}) collective-permute-start(bf16[130,512]{1,0:T(8,128)(2,1)S(1)} %get-tuple-element.9), channel_id=1, source_target_pairs={{0,64},{64,128},{128,192},{192,256},{256,320},{320,384},{384,448},... | collective-permute-start | bytes 399368 | tf_op jit(solution)/shard_map/ppermute | solution.py:190
  12.3 37.5 %collective-permute-start.1 = (bf16[130,512]{1,0:T(8,128)(2,1)S(1)}, bf16[130,512]{1,0:T(8,128)(2,1)S(1)}, u32[]{:S(2)}, u32[]{:S(2)}) collective-permute-start(bf16[130,512]{1,0:T(8,128)(2,1)S(1)} %get-tuple-element.10), channel_id=1, source_target_pairs={{64,0},{128,64},{192,128},{256,192},{320,256},{384,320},{448,384},... | collective-permute-start | bytes 399368 | tf_op jit(solution)/shard_map/ppermute | solution.py:192
  17.7 39.7 %all-to-all-start.2 = ((bf16[16,2,2560]{2,1,0:T(2,128)(2,1)}), bf16[16,2,2560]{2,1,0:T(2,128)(2,1)S(1)}, u32[]{:S(2)}, u32[]{:S(2)}) async-start(bf16[16,2,2560]{2,1,0:T(2,128)(2,1)} %reshape.193), calls=%async_computation.2 | async-start | bytes 327680 | tf_op jit(solution)/shard_map/all_to_all | solution.py:264
  54.5 15.2 %copy-start.5 = (f32[512]{0:T(512)S(1)}, f32[512]{0:T(512)}, u32[]{:S(2)}) copy-start(f32[512]{0:T(512)} %param.12) | copy-start | bytes 6148
  57.4 24.5 %all-to-all-start.1 = ((bf16[16,2,2560]{2,1,0:T(2,128)(2,1)}), bf16[16,2,2560]{2,1,0:T(2,128)(2,1)S(1)}, u32[]{:S(2)}, u32[]{:S(2)}) async-start(bf16[16,2,2560]{2,1,0:T(2,128)(2,1)} %reshape.195), calls=%async_computation.1 | async-start | bytes 327680 | tf_op jit(solution)/shard_map/all_to_all | solution.py:263
  81.8 19.5 %all-to-all-start = ((bf16[16,2,2560]{2,1,0:T(2,128)(2,1)}), bf16[16,2,2560]{2,1,0:T(2,128)(2,1)S(1)}, u32[]{:S(2)}, u32[]{:S(2)}) async-start(bf16[16,2,2560]{2,1,0:T(2,128)(2,1)} %reshape.191), calls=%async_computation | async-start | bytes 327680 | tf_op jit(solution)/shard_map/all_to_all | solution.py:262
  110.1 1.6 %copy-start.2 = (bf16[160,512]{1,0:T(8,128)(2,1)S(1)}, bf16[160,512]{1,0:T(8,128)(2,1)}, u32[]{:S(2)}) copy-start(bf16[160,512]{1,0:T(8,128)(2,1)} %concatenate.19) | copy-start | bytes 491524
  110.1 1.6 %copy-start.3 = (bf16[160,512]{1,0:T(8,128)(2,1)S(1)}, bf16[160,512]{1,0:T(8,128)(2,1)}, u32[]{:S(2)}) copy-start(bf16[160,512]{1,0:T(8,128)(2,1)} %concatenate.20) | copy-start | bytes 491524
Sparse Core Ops, SparseCore 0:
  9.5 39.8 all-gather.1

commit v2 on v1

v2 whole, which is shorter than its diff:
```python
import jax
import jax.numpy as jnp
from jax import lax
from jax.experimental import pallas as pl
from jax.experimental.pallas import tpu as pltpu
from jax.sharding import PartitionSpec as P

MESH = pl.DeviceIdType.MESH
F32 = jnp.float32
BF16 = jnp.bfloat16
EDGE = 144
BAND = 160
NEAR = 512
GROUP = 16
GROUPS = BAND // GROUP
ROWS = 16 * GROUP
TILE = (16, 128)


def dot(a, b):
    return lax.dot_general(a, b, (((1,), (0,)), ((), ())), preferred_element_type=F32)


def dot_nt(a, b):
    return lax.dot_general(a, b, (((1,), (1,)), ((), ())), preferred_element_type=F32)


def hidden_rows(near, inputs, local, taps):
    rows = inputs.shape[0]
    inputs = inputs.astype(F32)
    spatial = taps[0:1] * inputs
    column = lax.broadcasted_iota(jnp.int32, (rows, NEAR), 1)
    for k in range(8):
        pick = jnp.where(local[:, k : k + 1] == column, 1.0, 0.0).astype(BF16)
        spatial += taps[k + 1 : k + 2] * dot(pick, near)
    return (inputs + spatial).astype(BF16)


def normalized(hidden, gain):
    hidden = hidden.astype(F32)
    inverse = lax.rsqrt(jnp.mean(hidden * hidden, axis=-1, keepdims=True) + 1e-05)
    return (hidden * inverse * gain).astype(BF16)


def causal_bias():
    row = lax.broadcasted_iota(jnp.int32, (ROWS, ROWS), 0)
    col = lax.broadcasted_iota(jnp.int32, (ROWS, ROWS), 1)
    same = row % GROUP == col % GROUP
    return jnp.where(same & (col <= row), 0.0, -1e30).astype(F32)


def attend_pair(q, k, v, g, bias):
    lane = lax.broadcasted_iota(jnp.int32, q.shape, 1)
    sub = lax.broadcasted_iota(jnp.int32, q.shape[::-1], 0)
    q_t, v_t, g_t = q.T, v.T, g.T
    att_t = dq = dk_t = dv_t = 0.0
    for half in range(2):
        ours = lane // 64 == half
        ours_t = sub // 64 == half
        zero = jnp.zeros((), BF16)
        eighth = jnp.asarray(0.125, BF16)
        scores = dot_nt(jnp.where(ours, q * eighth, zero), k) + bias
        raised = jnp.exp(scores - jnp.max(scores, axis=-1, keepdims=True))
        weights = (raised * (1.0 / jnp.sum(raised, axis=-1, keepdims=True))).astype(BF16)
        dprob = dot_nt(jnp.where(ours, g, zero), v)
        wide = weights.astype(F32)
        delta = jnp.sum(wide * dprob, axis=-1, keepdims=True)
        dscore = (wide * (dprob - delta)).astype(BF16)
        att_t += dot_nt(jnp.where(ours_t, v_t, zero), weights)
        dq += dot(dscore, jnp.where(ours, k * eighth, zero))
        dk_t += dot(jnp.where(ours_t, q_t * eighth, zero), dscore)
        dv_t += dot(jnp.where(ours_t, g_t, zero), weights)
    return att_t.astype(BF16), dq.astype(BF16), dk_t.astype(BF16), dv_t.astype(BF16)


def group_of(zed, core):
    place = (zed + 16 - 2 * core) % 16
    group = (GROUPS * place + 15) // 16
    return jnp.minimum(group, GROUPS - 1), (16 * group) // GROUPS == place


def kernel(
    features,
    neighbours,
    taps,
    gain,
    qkv_shard,
    out_shard,
    cotangent,
    out,
    near,
    normed_out,
    normed_in,
    cot_in,
    qkv_all,
    out_all,
    projected,
    bias,
    att_t,
    dq_all,
    dkv_t,
    part,
    core_out,
    core_in,
    xs_out,
    xs_in,
    ys_out,
    ys_in,
    xs_sum,
    ys_sum,
    xs_out2,
    xs_in2,
    ys_out2,
    ys_in2,
    z_sum,
    z_out,
    z_in,
    halo_sems,
    weight_sems,
    cot_sems,
    normed_sems,
    core_sems,
    one_sems,
    two_sems,
    z_sems,
):
    blk = lax.axis_index("blk")
    zed = lax.axis_index("tm")
    fsdp = lax.axis_index("fsdp")
    x_lo, y = blk // 4, blk % 4
    x_hi, core = fsdp // 2, fsdp % 2
    x = x_hi * 2 + x_lo
    group, active = group_of(zed, core)

    def at_x(to):
        return ((to % 2) * 4 + y, zed, (to // 2) * 2 + core)

    def at_y(to):
        return (x_lo * 4 + to, zed, fsdp)

    def at_z(to):
        return (blk, to, fsdp)

    mate = (blk, zed, x_hi * 2 + 1 - core)
    facing = ((1 - x_lo) * 4 + y, zed, (1 - x_hi) * 2 + core)
    partners = [mate]
    partners += [at_x((x + d) % 4) for d in (1, 2, 3)]
    partners += [at_y((y + d) % 4) for d in (1, 2, 3)]
    partners += [at_z((zed + d) % 16) for d in range(1, 16)]
    barrier = pltpu.get_barrier_semaphore()

    def greet(to):
        pl.semaphore_signal(barrier, inc=1, device_id=to, device_id_type=MESH)

    for partner in partners:
        greet(partner)

    @pl.when(blk == 3)
    def _():
        greet((4, zed, fsdp))

    @pl.when(blk == 4)
    def _():
        greet((3, zed, fsdp))

    def remote(src, dst, sems, slot, to):
        return pltpu.make_async_remote_copy(
            src_ref=src,
            dst_ref=dst,
            send_sem=sems.at[0, slot],
            recv_sem=sems.at[1, slot],
            device_id=to,
            device_id_type=MESH,
        )

    def send(*args):
        copy = remote(*args)
        copy.start()
        return copy

    near[EDGE : EDGE + BAND] = features[...]
    near[2 * EDGE + BAND :] = jnp.zeros((NEAR - 2 * EDGE - BAND, 512), BF16)

    @pl.when(blk == 0)
    def _():
        near[0:EDGE] = jnp.zeros((EDGE, 512), BF16)

    @pl.when(blk == 7)
    def _():
        near[EDGE + BAND : 2 * EDGE + BAND] = jnp.zeros((EDGE, 512), BF16)

    @pl.when(active)
    def _():
        bias[...] = causal_bias()
        cot_in[zed] = cotangent[group]
    shard = pl.ds(pl.multiple_of(fsdp * 128, 128), 128)
    qkv_all[shard] = qkv_shard[...]
    out_all[shard] = out_shard[...]

    extra = jnp.where((blk == 3) | (blk == 4), 1, 0)
    pl.semaphore_wait(barrier, len(partners) + extra)

    up = remote(
        features.at[0:EDGE], near.at[EDGE + BAND : 2 * EDGE + BAND], halo_sems, 0,
        (jnp.maximum(blk - 1, 0), zed, fsdp),
    )
    down = remote(
        features.at[BAND - EDGE : BAND], near.at[0:EDGE], halo_sems, 1,
        (jnp.minimum(blk + 1, 7), zed, fsdp),
    )

    @pl.when(blk > 0)
    def _():
        up.start()

    @pl.when(blk < 7)
    def _():
        down.start()

    far_first = (8, 7, 9, 6, 10, 5, 11, 4, 12, 3, 13, 2, 14, 1, 15)

    def exchange(source, target, sems):
        copies = []
        for d in far_first:
            to = (zed + d) % 16
            theirs, wanted = group_of(to, core)
            copy = remote(source.at[theirs], target.at[zed], sems, d - 1, at_z(to))
            copies.append((copy, wanted))
            pl.when(wanted)(copy.start)
        return copies

    def arrivals(target, sems):
        for d in far_first:
            come = (zed + 16 - d) % 16
            remote(target.at[come], target.at[come], sems, d - 1, at_z(come)).wait_recv()

    cot_copies = exchange(cotangent, cot_in, cot_sems)
    weight_copies = [
        send(qkv_shard, qkv_all.at[shard], weight_sems, 0, facing),
        send(out_shard, out_all.at[shard], weight_sems, 1, facing),
        send(qkv_shard, qkv_all.at[shard], weight_sems, 2, mate),
        send(out_shard, out_all.at[shard], weight_sems, 3, mate),
    ]

    @pl.when(blk > 0)
    def _():
        down.wait_recv()

    @pl.when(blk < 7)
    def _():
        up.wait_recv()

    first_pixel = blk * BAND
    half_rows = BAND // 2
    for part_of in range(2):
        rows = slice(part_of * half_rows, (part_of + 1) * half_rows)
        local = neighbours[rows] - first_pixel + EDGE
        hidden = hidden_rows(near[...], features[rows], local, taps)
        groups = slice(part_of * GROUPS // 2, (part_of + 1) * GROUPS // 2)
        normed_out[groups] = normalized(hidden, gain[...]).reshape(GROUPS // 2, GROUP, 512)
    normed_copies = exchange(normed_out, normed_in, normed_sems)

    @pl.when(active)
    def _():
        normed_in[zed] = normed_out[group]

    facing_shard = pl.ds(pl.multiple_of(((1 - x_hi) * 2 + core) * 128, 128), 128)
    passed = [
        (qkv_all.at[facing_shard], weight_sems, 4, mate),
        (out_all.at[facing_shard], weight_sems, 5, mate),
    ]
    weight_copies[0].wait_recv()
    weight_copies[1].wait_recv()
    weight_copies += [send(ref, ref, sems, slot, to) for ref, sems, slot, to in passed]
    for copy in weight_copies[2:]:
        copy.wait_recv()

    @pl.when(active)
    def _():
        arrivals(cot_in, cot_sems)
        cots = cot_in[...].reshape(ROWS, 512)
        grads = dot_nt(cots, out_all[...]).astype(BF16)
        arrivals(normed_in, normed_sems)
        normed = normed_in[...].reshape(ROWS, 512)
        for j in range(6):
            block = slice(256 * j, 256 * j + 256)
            projected[:, block] = dot(normed, qkv_all[:, block]).astype(BF16)
        for pair in range(4):
            cols = slice(128 * pair, 128 * pair + 128)
            att, dq, dk, dv = attend_pair(
                projected[:, 128 * pair : 128 * pair + 128],
                projected[:, 512 + 128 * pair : 640 + 128 * pair],
                projected[:, 1024 + 128 * pair : 1152 + 128 * pair],
                grads[:, cols],
                bias[...],
            )
            att_t[cols] = att
            dq_all[:, cols] = dq
            dkv_t[128 * pair : 128 * pair + 128] = dk
            dkv_t[512 + 128 * pair : 640 + 128 * pair] = dv
        normed_t = normed.T
        for r in range(4):
            rows = slice(128 * r, 128 * r + 128)
            grad_q = dot(normed_t[rows], dq_all[...])
            grad_kv = dot_nt(normed_t[rows], dkv_t[...])
            for j in range(12):
                block = grad_q if j < 4 else grad_kv
                at = j if j < 4 else j - 4
                part[pl.ds(1536 * r + j, 128, stride=12), :] = block[:, 128 * at : 128 * at + 128]
            grad_o = dot(att_t[rows], cots)
            for j in range(4):
                part[pl.ds(6144 + 512 * r + j, 128, stride=4), :] = grad_o[
                    :, 128 * j : 128 * j + 128
                ]

    @pl.when(jnp.logical_not(active))
    def _():
        part[...] = jnp.zeros_like(part)

    def chunks(lo, j, first, count, hi, c):
        start = (((lo * 4 + j) * 16 + first) * 4 + hi * 2 + c) * 16
        return jnp.stack(
            [part[pl.ds(pl.multiple_of(start + i * 64, 16), 16), :] for i in range(count)]
        )

    for hi in range(2):
        for lo in range(2):
            for j in range(4):
                core_out[hi * 2 + lo, j] = chunks(lo, j, 0, 16, hi, 1 - core).astype(BF16)
    first = send(core_out, core_in, core_sems, 0, mate)
    first.wait()

    for hi in range(2):
        for lo in range(2):
            for j in range(4):
                total = chunks(lo, j, 0, 16, hi, core) + core_in[hi * 2 + lo, j].astype(F32)
                xs_out[hi * 2 + lo, j] = total[:8].astype(BF16)
                ys_out[j, hi * 2 + lo] = total[8:].astype(BF16)
    ones = []
    for d in (2, 1, 3):
        to = (x + d) % 4
        ones.append(send(xs_out.at[to], xs_in.at[d - 1], one_sems, d - 1, at_x(to)))
        to = (y + d) % 4
        ones.append(send(ys_out.at[to], ys_in.at[d - 1], one_sems, d + 2, at_y(to)))
    for j in range(4):
        xs_sum[j] = chunks(x_lo, j, 0, 8, x_hi, core) + core_in[x, j, 0:8].astype(F32)
        ys_sum[j] = chunks(j % 2, y, 8, 8, j // 2, core) + core_in[j, y, 8:16].astype(F32)
    for copy in ones:
        copy.wait_recv()
    for j in range(4):
        total = xs_sum[j]
        for d in range(3):
            total += xs_in[d, j].astype(F32)
        xs_sum[j] = total
        xs_out2[j] = total.astype(BF16)
        total = ys_sum[j]
        for d in range(3):
            total += ys_in[d, j].astype(F32)
        ys_sum[j] = total
        ys_out2[j] = total.astype(BF16)
    twos = []
    for d in (2, 1, 3):
        to = (y + d) % 4
        twos.append(send(xs_out2.at[to], xs_in2.at[d - 1], two_sems, d - 1, at_y(to)))
        to = (x + d) % 4
        twos.append(send(ys_out2.at[to], ys_in2.at[d - 1], two_sems, d + 2, at_x(to)))
    for copy in twos:
        copy.wait_recv()
    low, high = xs_sum[y], ys_sum[x]
    for d in range(3):
        low += xs_in2[d].astype(F32)
        high += ys_in2[d].astype(F32)
    z_sum[0:8] = low
    z_sum[8:16] = high
    z_out[0:8] = low.astype(BF16)
    z_out[8:16] = high.astype(BF16)
    threes = []
    for d in far_first:
        to = (zed + d) % 16
        threes.append(send(z_out.at[to], z_in.at[d - 1], z_sems, d - 1, at_z(to)))
    for copy in threes:
        copy.wait_recv()
    total = z_sum[zed]
    for d in range(15):
        total += z_in[d].astype(F32)
    out[...] = total

    for copy in weight_copies + ones + twos + threes:
        copy.wait_send()
    for copy, wanted in cot_copies + normed_copies:
        pl.when(wanted)(copy.wait_send)

    @pl.when(blk > 0)
    def _():
        up.wait_send()

    @pl.when(blk < 7)
    def _():
        down.wait_send()


def per_device(features, neighbours, conv_taps, norm_gain, qkv_weight, out_weight, cotangent):
    vmem = pl.BlockSpec(memory_space=pltpu.VMEM)

    def pair(count):
        return pltpu.SemaphoreType.DMA((2, count))

    result = pl.pallas_call(
        kernel,
        out_shape=jax.ShapeDtypeStruct(TILE, F32),
        in_specs=[vmem] * 7,
        out_specs=vmem,
        scratch_shapes=[
            pltpu.VMEM((NEAR, 512), BF16),
            pltpu.VMEM((GROUPS, GROUP, 512), BF16),
            pltpu.VMEM((16, GROUP, 512), BF16),
            pltpu.VMEM((16, GROUP, 512), BF16),
            pltpu.VMEM((512, 1536), BF16),
            pltpu.VMEM((512, 512), BF16),
            pltpu.VMEM((ROWS, 1536), BF16),
            pltpu.VMEM((ROWS, ROWS), F32),
            pltpu.VMEM((512, ROWS), BF16),
            pltpu.VMEM((ROWS, 512), BF16),
            pltpu.VMEM((1024, ROWS), BF16),
            pltpu.VMEM((8192, 128), F32),
            pltpu.VMEM((4, 4, 16) + TILE, BF16),
            pltpu.VMEM((4, 4, 16) + TILE, BF16),
            pltpu.VMEM((4, 4, 8) + TILE, BF16),
            pltpu.VMEM((3, 4, 8) + TILE, BF16),
            pltpu.VMEM((4, 4, 8) + TILE, BF16),
            pltpu.VMEM((3, 4, 8) + TILE, BF16),
            pltpu.VMEM((4, 8) + TILE, F32),
            pltpu.VMEM((4, 8) + TILE, F32),
            pltpu.VMEM((4, 8) + TILE, BF16),
            pltpu.VMEM((3, 8) + TILE, BF16),
            pltpu.VMEM((4, 8) + TILE, BF16),
            pltpu.VMEM((3, 8) + TILE, BF16),
            pltpu.VMEM((16,) + TILE, F32),
            pltpu.VMEM((16,) + TILE, BF16),
            pltpu.VMEM((15,) + TILE, BF16),
            pair(2),
            pair(6),
            pair(15),
            pair(15),
            pair(1),
            pair(6),
            pair(6),
            pair(15),
        ],
        compiler_params=pltpu.CompilerParams(
            collective_id=0, has_side_effects=True, vmem_limit_bytes=48 * 1024 * 1024
        ),
    )(
        features.reshape(BAND, 512),
        neighbours,
        conv_taps,
        norm_gain.reshape(1, 512),
        qkv_weight,
        out_weight,
        cotangent.reshape(GROUPS, GROUP, 512),
    )
    return result.reshape(-1)


def solution(mesh):
    return jax.shard_map(
        per_device,
        mesh=mesh,
        in_specs=(
            P("fsdp", "tm", "blk", None),
            P("blk", None),
            P(),
            P(),
            P("fsdp", None),
            P("fsdp", None),
            P("fsdp", "tm", "blk", None),
        ),
        out_specs=P(("blk", "tm", "fsdp")),
        check_vma=False,
    )
```

time: 160 us -> 68.2 us (0.43)
  starting transfers between devices: 39.3 us -> 0 us
  Pallas kernels: 33.9 us -> 62.3 us
  waiting for transfers between devices: 20.9 us -> 0 us
  local copies, waits for them, and re-layouts: 22.3 us -> 5.13 us
  between operations: 13.9 us -> 0.05 us
  blocking collectives: 13.2 us -> 0 us
  other arithmetic: 9.53 us -> 0 us
  matrix products: 5.87 us -> 0 us
    all_to_all x3 -> x0, starting transfers between devices: 34 us -> none  [the longest x1 14.9 us: per_device(): lax.all_to_all(upstream[None], 'tm', split_axis=1, concat_axis=0, tiled=T...]
    pallas_call x1, Pallas kernels: 33.9 us -> 62.3 us  [per_device(): pl.pallas_call(kernel, out_shape=jax.ShapeDtypeStruct(TILE, F32), in_spec...]
    all_to_all x3 -> x0, waiting for transfers between devices: 20.2 us -> none  [the longest x1 10.8 us: per_device(): lax.all_to_all(normed[None], 'tm', split_axis=1, concat_axis=0, tiled=True)]
    all_gather x1 -> x0, blocking collectives: 13.2 us -> none  [per_device(): lax.all_gather(out_weight, 'fsdp', axis=0, tiled=True)]
    gather x8 -> x0, local copies, waits for them, and re-layouts: 7.45 us -> none  [per_device(): jnp.take(padded, local_rows[:, column], axis=0).astype(jnp.float32)]
    dot_general x10 -> x0, matrix products: 5.87 us -> none  [the longest x1 1.83 us: per_device(): jnp.dot(flat_normed, full_qkv, preferred_element_type=jnp.float32)]
    ppermute x2 -> x0, starting transfers between devices: 5.33 us -> none  [the longest x1 4.04 us: with_halo(): lax.ppermute(tail, axis, [(i, (i + 1) % count) for i in range(ends)])]
    unnamed x3 -> x0, other arithmetic: 4.8 us -> none
  transfers between devices with their start and end apart: 6 -> 0, of which waited for: 2 -> 0; matrix products, arithmetic and copies ran while one was open for 13% -> 0% of each run, Pallas kernels for 0% -> 0%
where the time goes in v2:
time: 68.2 us; the launch traced here: 67.5 us
  Pallas kernels  62.3 us (91%)
  local copies, waits for them, and re-layouts  5.13 us (8%)
    pallas_call x1, Pallas kernels, per_device(): pl.pallas_call(kernel, out_shape=jax.ShapeDtypeStruct(TILE, F32), in_spec...  62.3 us
    unnamed x14, local copies, waits for them, and re-layouts  5.13 us

profile of v2, /device:TPU:1, one launch (start us, length us, event | category | flops | bytes accessed | tf_op | source)
XLA Modules:
  0.0 67.5 jit_solution(8305771935345936954)
XLA Ops:
  0.0 0.0 copy-start.4
  0.0 0.0 copy-start.5
  0.0 0.8 %copy.8.neighbours = s32[160,8]{1,0:T(8,128)S(1)} copy(s32[160,8]{0,1:T(8,128)} %param.8) | data formatting | bytes 10240 | tf_op args[1]
  0.8 0.0 copy-done.4
  0.8 0.0 copy-done.5
  0.8 0.0 copy-start
  0.8 1.0 %copy-done = bf16[128,1536]{1,0:T(8,128)(2,1)S(1)} copy-done((bf16[128,1536]{1,0:T(8,128)(2,1)S(1)}, bf16[128,1536]{1,0:T(8,128)(2,1)}, u32[]{:S(2)}) %copy-start) | copy-done | bytes 393240
  1.8 0.0 copy-start.1
  1.8 0.9 %copy-done.1 = bf16[1,1,160,512]{3,2,1,0:T(8,128)(2,1)S(1)} copy-done((bf16[1,1,160,512]{3,2,1,0:T(8,128)(2,1)S(1)}, bf16[1,1,160,512]{3,2,1,0:T(8,128)(2,1)}, u32[]{:S(2)}) %copy-start.1) | copy-done | bytes 163864
  2.7 0.0 copy-start.2
  2.7 0.9 %copy-done.2 = bf16[1,1,160,512]{3,2,1,0:T(8,128)(2,1)S(1)} copy-done((bf16[1,1,160,512]{3,2,1,0:T(8,128)(2,1)S(1)}, bf16[1,1,160,512]{3,2,1,0:T(8,128)(2,1)}, u32[]{:S(2)}) %copy-start.2) | copy-done | bytes 163864
  3.7 0.0 copy-start.3
  3.7 0.9 %copy-done.3 = bf16[128,512]{1,0:T(8,128)(2,1)S(1)} copy-done((bf16[128,512]{1,0:T(8,128)(2,1)S(1)}, bf16[128,512]{1,0:T(8,128)(2,1)}, u32[]{:S(2)}) %copy-start.3) | copy-done | bytes 131096
  4.6 62.3 %shard_map.73 = f32[16,128]{1,0:T(8,128)S(1)} custom-call(bf16[160,512]{1,0:T(8,128)(2,1)S(1)} %bitcast.4, s32[160,8]{1,0:T(8,128)S(1)} %copy.8.neighbours, f32[9,512]{1,0:T(8,128)S(1)} %copy-done.4, f32[1,512]{1,0:T(1,128)S(1)} %bitcast.7, bf16[128,1536]{1,0:T(8,128)(2,1)S(1)} %copy-done, bf16[128,512]{1,0:T(8,128)(2,1)S(1)} %copy-done.3, ...), custom_call_target="tpu_custom_call" | custom-call | tf_op jit(solution)/shard_map/pallas_call | solution.py:408
  66.9 0.6 copy.10
Async XLA Ops:
  0.0 0.8 %copy-start.4 = (f32[9,512]{1,0:T(8,128)S(1)}, f32[9,512]{1,0:T(8,128)}, u32[]{:S(2)}) copy-start(f32[9,512]{1,0:T(8,128)} %taps.1) | copy-start | bytes 55300
  0.0 0.8 %copy-start.5 = (f32[512]{0:T(512)S(1)}, f32[512]{0:T(512)}, u32[]{:S(2)}) copy-start(f32[512]{0:T(512)} %param.10) | copy-start | bytes 6148
  0.8 1.0 %copy-start = (bf16[128,1536]{1,0:T(8,128)(2,1)S(1)}, bf16[128,1536]{1,0:T(8,128)(2,1)}, u32[]{:S(2)}) copy-start(bf16[128,1536]{1,0:T(8,128)(2,1)} %qkv_shard.1) | copy-start | bytes 1179652
  1.8 0.9 %copy-start.1 = (bf16[1,1,160,512]{3,2,1,0:T(8,128)(2,1)S(1)}, bf16[1,1,160,512]{3,2,1,0:T(8,128)(2,1)}, u32[]{:S(2)}) copy-start(bf16[1,1,160,512]{3,2,1,0:T(8,128)(2,1)} %param.7) | copy-start | bytes 491524
  2.7 0.9 %copy-start.2 = (bf16[1,1,160,512]{3,2,1,0:T(8,128)(2,1)S(1)}, bf16[1,1,160,512]{3,2,1,0:T(8,128)(2,1)}, u32[]{:S(2)}) copy-start(bf16[1,1,160,512]{3,2,1,0:T(8,128)(2,1)} %param.13) | copy-start | bytes 491524
  3.7 0.9 %copy-start.3 = (bf16[128,512]{1,0:T(8,128)(2,1)S(1)}, bf16[128,512]{1,0:T(8,128)(2,1)}, u32[]{:S(2)}) copy-start(bf16[128,512]{1,0:T(8,128)(2,1)} %out_shard.1) | copy-start | bytes 393220

commit v3 on v2

v3 whole, which is shorter than its diff:
```python
import jax
import jax.numpy as jnp
from jax import lax
from jax.experimental import pallas as pl
from jax.experimental.pallas import tpu as pltpu
from jax.sharding import PartitionSpec as P

MESH = pl.DeviceIdType.MESH
F32 = jnp.float32
BF16 = jnp.bfloat16
EDGE = 144
BAND = 160
NEAR = 512
GROUP = 16
GROUPS = BAND // GROUP
ROWS = 16 * GROUP
TILE = (16, 128)


def dot(a, b):
    return lax.dot_general(a, b, (((1,), (0,)), ((), ())), preferred_element_type=F32)


def dot_nt(a, b):
    return lax.dot_general(a, b, (((1,), (1,)), ((), ())), preferred_element_type=F32)


def hidden_rows(near, inputs, local, taps):
    rows = inputs.shape[0]
    inputs = inputs.astype(F32)
    spatial = taps[0:1] * inputs
    column = lax.broadcasted_iota(jnp.int32, (rows, NEAR), 1)
    for k in range(8):
        pick = jnp.where(local[:, k : k + 1] == column, 1.0, 0.0).astype(BF16)
        spatial += taps[k + 1 : k + 2] * dot(pick, near)
    return (inputs + spatial).astype(BF16)


def normalized(hidden, gain):
    hidden = hidden.astype(F32)
    inverse = lax.rsqrt(jnp.mean(hidden * hidden, axis=-1, keepdims=True) + 1e-05)
    return (hidden * inverse * gain).astype(BF16)


def causal_bias():
    row = lax.broadcasted_iota(jnp.int32, (ROWS, ROWS), 0)
    col = lax.broadcasted_iota(jnp.int32, (ROWS, ROWS), 1)
    same = row % GROUP == col % GROUP
    return jnp.where(same & (col <= row), 0.0, -1e30).astype(F32)


def attend_pair(q, k, v, g, bias):
    lane = lax.broadcasted_iota(jnp.int32, q.shape, 1)
    sub = lax.broadcasted_iota(jnp.int32, q.shape[::-1], 0)
    q_t, v_t, g_t = q.T, v.T, g.T
    att_t = dq = dk_t = dv_t = 0.0
    for half in range(2):
        ours = lane // 64 == half
        ours_t = sub // 64 == half
        zero = jnp.zeros((), BF16)
        eighth = jnp.asarray(0.125, BF16)
        scores = dot_nt(jnp.where(ours, q * eighth, zero), k) + bias
        raised = jnp.exp(scores - jnp.max(scores, axis=-1, keepdims=True))
        weights = (raised * (1.0 / jnp.sum(raised, axis=-1, keepdims=True))).astype(BF16)
        dprob = dot_nt(jnp.where(ours, g, zero), v)
        wide = weights.astype(F32)
        delta = jnp.sum(wide * dprob, axis=-1, keepdims=True)
        dscore = (wide * (dprob - delta)).astype(BF16)
        att_t += dot_nt(jnp.where(ours_t, v_t, zero), weights)
        dq += dot(dscore, jnp.where(ours, k * eighth, zero))
        dk_t += dot(jnp.where(ours_t, q_t * eighth, zero), dscore)
        dv_t += dot(jnp.where(ours_t, g_t, zero), weights)
    return att_t.astype(BF16), dq.astype(BF16), dk_t.astype(BF16), dv_t.astype(BF16)


def place_of(group):
    return (16 * group) // GROUPS


def group_of(zed):
    group = jnp.minimum((GROUPS * zed + 15) // 16, GROUPS - 1)
    return group, place_of(group) == zed


def kernel(
    features,
    neighbours,
    taps_in,
    gain_in,
    qkv_shard,
    out_shard,
    cotangent,
    out,
    near,
    nearby,
    taps,
    gain,
    normed_out,
    normed_in,
    cot_in,
    qkv_all,
    out_all,
    projected,
    bias,
    att_t,
    dq_all,
    dkv_t,
    part,
    core_out,
    core_in,
    out_1,
    in_1,
    sum_1,
    out_2,
    in_2,
    z_sum,
    z_out,
    z_in,
    local_sems,
    halo_sems,
    weight_sems,
    cot_sems,
    normed_sems,
    core_sems,
    one_sems,
    two_sems,
    z_sems,
):
    blk = lax.axis_index("blk")
    zed = lax.axis_index("tm")
    fsdp = lax.axis_index("fsdp")
    x_lo, y = blk // 4, blk % 4
    x_hi, core = fsdp // 2, fsdp % 2
    x = x_hi * 2 + x_lo
    group, active = group_of(zed)

    def at_x(to):
        return ((to % 2) * 4 + y, zed, (to // 2) * 2 + core)

    def at_y(to):
        return (x_lo * 4 + to, zed, fsdp)

    def at_z(to):
        return (blk, to, fsdp)

    mate = (blk, zed, x_hi * 2 + 1 - core)
    facing = ((1 - x_lo) * 4 + y, zed, (1 - x_hi) * 2 + core)
    partners = [mate]
    partners += [at_x((x + d) % 4) for d in (1, 2, 3)]
    partners += [at_y((y + d) % 4) for d in (1, 2, 3)]
    partners += [at_z((zed + d) % 16) for d in range(1, 16)]
    barrier = pltpu.get_barrier_semaphore()

    def greet(to):
        pl.semaphore_signal(barrier, inc=1, device_id=to, device_id_type=MESH)

    for partner in partners:
        greet(partner)

    @pl.when(blk == 3)
    def _():
        greet((4, zed, fsdp))

    @pl.when(blk == 4)
    def _():
        greet((3, zed, fsdp))

    def remote(src, dst, send_sem, recv_sem, to):
        return pltpu.make_async_remote_copy(
            src_ref=src,
            dst_ref=dst,
            send_sem=send_sem,
            recv_sem=recv_sem,
            device_id=to,
            device_id_type=MESH,
        )

    def send(src, dst, sems, slot, to):
        copy = remote(src, dst, sems.at[0, slot], sems.at[1, slot], to)
        copy.start()
        return copy

    shard = pl.ds(pl.multiple_of(fsdp * 128, 128), 128)
    owned = [
        pltpu.make_async_copy(src, dst, local_sems.at[i])
        for i, (src, dst) in enumerate(
            (
                (features, near.at[EDGE : EDGE + BAND]),
                (neighbours, nearby),
                (taps_in, taps),
                (gain_in, gain),
            )
        )
    ]
    held = [
        pltpu.make_async_copy(src, dst, local_sems.at[4 + i])
        for i, (src, dst) in enumerate(
            (
                (cotangent.at[group], cot_in.at[zed]),
                (qkv_shard, qkv_all.at[shard]),
                (out_shard, out_all.at[shard]),
            )
        )
    ]
    for copy in owned:
        copy.start()

    @pl.when(active)
    def _():
        for copy in held:
            copy.start()

    near[2 * EDGE + BAND :] = jnp.zeros((NEAR - 2 * EDGE - BAND, 512), BF16)
    z_in[...] = jnp.zeros_like(z_in)

    @pl.when(blk == 0)
    def _():
        near[0:EDGE] = jnp.zeros((EDGE, 512), BF16)

    @pl.when(blk == 7)
    def _():
        near[EDGE + BAND : 2 * EDGE + BAND] = jnp.zeros((EDGE, 512), BF16)

    @pl.when(active)
    def _():
        bias[...] = causal_bias()

    @pl.when(jnp.logical_not(active))
    def _():
        z_sum[...] = jnp.zeros_like(z_sum)

    for copy in owned:
        copy.wait()

    extra = jnp.where((blk == 3) | (blk == 4), 1, 0)
    pl.semaphore_wait(barrier, len(partners) + extra)

    up = remote(
        near.at[EDGE : 2 * EDGE],
        near.at[EDGE + BAND : 2 * EDGE + BAND],
        halo_sems.at[0, 0],
        halo_sems.at[1, 0],
        (jnp.maximum(blk - 1, 0), zed, fsdp),
    )
    down = remote(
        near.at[BAND : EDGE + BAND],
        near.at[0:EDGE],
        halo_sems.at[0, 1],
        halo_sems.at[1, 1],
        (jnp.minimum(blk + 1, 7), zed, fsdp),
    )

    @pl.when(blk > 0)
    def _():
        up.start()

    @pl.when(blk < 7)
    def _():
        down.start()

    def exchange(source, target, sems, first, count):
        copies = []
        for k in range(count):
            theirs = first + (k + zed) % count
            to = place_of(theirs)
            copy = remote(
                source.at[theirs], target.at[zed], sems.at[0, theirs], sems.at[1, zed], at_z(to)
            )
            other = to != zed
            copies.append((copy, other))
            pl.when(other)(copy.start)
        return copies

    def arrivals(target, sems):
        for come in range(16):
            copy = remote(
                target.at[come], target.at[come], sems.at[0, 0], sems.at[1, come], at_z(come)
            )
            pl.when(come != zed)(copy.wait_recv)

    weight_copies = [
        remote(src, dst.at[shard], weight_sems.at[0, i], weight_sems.at[1, i], to)
        for i, (src, dst, to) in enumerate(
            (
                (qkv_shard, qkv_all, facing),
                (out_shard, out_all, facing),
                (qkv_shard, qkv_all, mate),
                (out_shard, out_all, mate),
            )
        )
    ]

    @pl.when(active)
    def _():
        for copy in weight_copies:
            copy.start()

    cot_copies = exchange(cotangent, cot_in, cot_sems, 0, GROUPS)
    local_all = nearby[...].T - (blk * BAND - EDGE)

    @pl.when(blk > 0)
    def _():
        down.wait_recv()

    @pl.when(blk < 7)
    def _():
        up.wait_recv()

    normed_copies = []
    half_rows, half_groups = BAND // 2, GROUPS // 2
    for half in range(2):
        rows = slice(half * half_rows, (half + 1) * half_rows)
        own = near[EDGE + half * half_rows : EDGE + (half + 1) * half_rows]
        hidden = hidden_rows(near[...], own, local_all[rows], taps)
        normed_out[half * half_groups : (half + 1) * half_groups] = normalized(
            hidden, gain[...]
        ).reshape(half_groups, GROUP, 512)
        normed_copies += exchange(
            normed_out, normed_in, normed_sems, half * half_groups, half_groups
        )

    @pl.when(active)
    def _():
        normed_in[zed] = normed_out[group]
        facing_shard = pl.ds(pl.multiple_of(((1 - x_hi) * 2 + core) * 128, 128), 128)
        weight_copies[0].wait_recv()
        weight_copies[1].wait_recv()
        passed = [
            send(qkv_all.at[facing_shard], qkv_all.at[facing_shard], weight_sems, 4, mate),
            send(out_all.at[facing_shard], out_all.at[facing_shard], weight_sems, 5, mate),
        ]
        for copy in held:
            copy.wait()
        for copy in weight_copies[2:] + passed:
            copy.wait_recv()
        arrivals(cot_in, cot_sems)
        cots = cot_in[...].reshape(ROWS, 512)
        grads = dot_nt(cots, out_all[...]).astype(BF16)
        arrivals(normed_in, normed_sems)
        normed = normed_in[...].reshape(ROWS, 512)
        for j in range(6):
            block = slice(256 * j, 256 * j + 256)
            projected[:, block] = dot(normed, qkv_all[:, block]).astype(BF16)
        for pair in range(4):
            cols = slice(128 * pair, 128 * pair + 128)
            att, dq, dk, dv = attend_pair(
                projected[:, 128 * pair : 128 * pair + 128],
                projected[:, 512 + 128 * pair : 640 + 128 * pair],
                projected[:, 1024 + 128 * pair : 1152 + 128 * pair],
                grads[:, cols],
                bias[...],
            )
            att_t[cols] = att
            dq_all[:, cols] = dq
            dkv_t[128 * pair : 128 * pair + 128] = dk
            dkv_t[512 + 128 * pair : 640 + 128 * pair] = dv
        normed_t = normed.T
        for r in range(4):
            rows = slice(128 * r, 128 * r + 128)
            grad_q = dot(normed_t[rows], dq_all[...])
            grad_kv = dot_nt(normed_t[rows], dkv_t[...])
            for j in range(12):
                block = grad_q if j < 4 else grad_kv
                at = j if j < 4 else j - 4
                part[pl.ds(1536 * r + j, 128, stride=12), :] = block[:, 128 * at : 128 * at + 128]
            grad_o = dot(att_t[rows], cots)
            for j in range(4):
                part[pl.ds(6144 + 512 * r + j, 128, stride=4), :] = grad_o[
                    :, 128 * j : 128 * j + 128
                ]

        def chunks(at_chip_x, at_chip_y, piece, c):
            blk_of = (at_chip_x % 2) * 4 + at_chip_y
            start = ((blk_of * 16 + 4 * piece) * 4 + (at_chip_x // 2) * 2 + c) * 16
            return jnp.stack(
                [part[pl.ds(pl.multiple_of(start + i * 64, 16), 16), :] for i in range(4)]
            )

        def piece_chunks(piece, first, second, c):
            if piece % 2 == 0:
                return chunks(first, second, piece, c)
            return chunks(second, first, piece, c)

        def along(piece, first):
            if (piece % 2 == 0) == first:
                return x, at_x
            return y, at_y

        zeros, ones, twos, threes = [], [], [], []
        for i in range(4):
            for p in range(4):
                for q in range(4):
                    core_out[i, p, q] = piece_chunks(i, p, q, 1 - core).astype(BF16)
            zeros.append(send(core_out.at[i], core_in.at[i], core_sems, i, mate))
        for i in range(4):
            zeros[i].wait_recv()
            for p in range(4):
                for q in range(4):
                    total = piece_chunks(i, p, q, core) + core_in[i, p, q].astype(F32)
                    out_1[i, p, q] = total.astype(BF16)
            here, at = along(i, True)
            for d in (2, 1, 3):
                to = (here + d) % 4
                ones.append(
                    send(out_1.at[i, to], in_1.at[i, d - 1], one_sems, 3 * i + d - 1, at(to))
                )
            for q in range(4):
                sum_1[i, q] = piece_chunks(i, here, q, core) + core_in[i, here, q].astype(F32)
        for i in range(4):
            for copy in ones[3 * i : 3 * i + 3]:
                copy.wait_recv()
            for q in range(4):
                total = sum_1[i, q]
                for d in range(3):
                    total += in_1[i, d, q].astype(F32)
                sum_1[i, q] = total
                out_2[i, q] = total.astype(BF16)
            here, at = along(i, False)
            for d in (2, 1, 3):
                to = (here + d) % 4
                twos.append(
                    send(out_2.at[i, to], in_2.at[i, d - 1], two_sems, 3 * i + d - 1, at(to))
                )
        for i in range(4):
            for copy in twos[3 * i : 3 * i + 3]:
                copy.wait_recv()
            here, at = along(i, False)
            total = sum_1[i, here]
            for d in range(3):
                total += in_2[i, d].astype(F32)
            z_sum[4 * i : 4 * i + 4] = total
            z_out[4 * i : 4 * i + 4] = total.astype(BF16)
            for k in range(4):
                to = 4 * i + (k + zed) % 4
                copy = remote(
                    z_out.at[to], z_in.at[zed], z_sems.at[0, to], z_sems.at[1, zed], at_z(to)
                )
                other = to != zed
                pl.when(other)(copy.start)
                threes.append((copy, other))

        for copy in weight_copies + passed + zeros + ones + twos:
            copy.wait_send()
        for copy, other in threes:
            pl.when(other)(copy.wait_send)

    total = z_sum[zed]
    for g in range(GROUPS):
        come = place_of(g)
        copy = remote(
            z_in.at[come], z_in.at[come], z_sems.at[0, 0], z_sems.at[1, come], at_z(come)
        )
        pl.when(come != zed)(copy.wait_recv)
    for g in range(GROUPS):
        total += z_in[place_of(g)].astype(F32)
    out[...] = total

    for copy, other in cot_copies + normed_copies:
        pl.when(other)(copy.wait_send)

    @pl.when(blk > 0)
    def _():
        up.wait_send()

    @pl.when(blk < 7)
    def _():
        down.wait_send()


def per_device(features, neighbours, conv_taps, norm_gain, qkv_weight, out_weight, cotangent):
    def pair(count):
        return pltpu.SemaphoreType.DMA((2, count))

    result = pl.pallas_call(
        kernel,
        out_shape=jax.ShapeDtypeStruct(TILE, F32),
        in_specs=[pl.BlockSpec(memory_space=pltpu.HBM)] * 7,
        out_specs=pl.BlockSpec(memory_space=pltpu.VMEM),
        scratch_shapes=[
            pltpu.VMEM((NEAR, 512), BF16),
            pltpu.VMEM((8, BAND), jnp.int32),
            pltpu.VMEM((9, 512), F32),
            pltpu.VMEM((1, 512), F32),
            pltpu.VMEM((GROUPS, GROUP, 512), BF16),
            pltpu.VMEM((16, GROUP, 512), BF16),
            pltpu.VMEM((16, GROUP, 512), BF16),
            pltpu.VMEM((512, 1536), BF16),
            pltpu.VMEM((512, 512), BF16),
            pltpu.VMEM((ROWS, 1536), BF16),
            pltpu.VMEM((ROWS, ROWS), F32),
            pltpu.VMEM((512, ROWS), BF16),
            pltpu.VMEM((ROWS, 512), BF16),
            pltpu.VMEM((1024, ROWS), BF16),
            pltpu.VMEM((8192, 128), F32),
            pltpu.VMEM((4, 4, 4, 4) + TILE, BF16),
            pltpu.VMEM((4, 4, 4, 4) + TILE, BF16),
            pltpu.VMEM((4, 4, 4, 4) + TILE, BF16),
            pltpu.VMEM((4, 3, 4, 4) + TILE, BF16),
            pltpu.VMEM((4, 4, 4) + TILE, F32),
            pltpu.VMEM((4, 4, 4) + TILE, BF16),
            pltpu.VMEM((4, 3, 4) + TILE, BF16),
            pltpu.VMEM((16,) + TILE, F32),
            pltpu.VMEM((16,) + TILE, BF16),
            pltpu.VMEM((16,) + TILE, BF16),
            pltpu.SemaphoreType.DMA((7,)),
            pair(2),
            pair(6),
            pair(16),
            pair(16),
            pair(4),
            pair(12),
            pair(12),
            pair(16),
        ],
        compiler_params=pltpu.CompilerParams(
            collective_id=0, has_side_effects=True, vmem_limit_bytes=60 * 1024 * 1024
        ),
    )(
        features.reshape(BAND, 512),
        neighbours.T,
        conv_taps,
        norm_gain.reshape(1, 512),
        qkv_weight,
        out_weight,
        cotangent.reshape(GROUPS, GROUP, 512),
    )
    return result.reshape(-1)


def solution(mesh):
    return jax.shard_map(
        per_device,
        mesh=mesh,
        in_specs=(
            P("fsdp", "tm", "blk", None),
            P("blk", None),
            P(),
            P(),
            P("fsdp", None),
            P("fsdp", None),
            P("fsdp", "tm", "blk", None),
        ),
        out_specs=P(("blk", "tm", "fsdp")),
        check_vma=False,
    )
```

time: 68.2 us -> 62.4 us (0.915)
  local copies, waits for them, and re-layouts: 5.13 us -> 1.3 us
  Pallas kernels: 62.3 us -> 60.6 us
    unnamed x14 -> x1, local copies, waits for them, and re-layouts: 5.13 us -> 1.3 us
    pallas_call x1, Pallas kernels: 62.3 us -> 60.6 us  [per_device(): pl.pallas_call(kernel, out_shape=jax.ShapeDtypeStruct(TILE, F32), in_spec...]
where the time goes in v3:
time: 62.4 us; the launch traced here: 61.9 us
  Pallas kernels  60.6 us (97%)
  local copies, waits for them, and re-layouts  1.3 us (2%)
    pallas_call x1, Pallas kernels, per_device(): pl.pallas_call(kernel, out_shape=jax.ShapeDtypeStruct(TILE, F32), in_spec...  60.6 us
    unnamed x1, local copies, waits for them, and re-layouts  1.3 us

profile of v3, /device:TPU:1, one launch (start us, length us, event | category | flops | bytes accessed | tf_op | source)
XLA Modules:
  0.0 61.9 jit_solution(17090624796822034884)
XLA Ops:
  0.0 60.6 %shard_map.73 = f32[16,128]{1,0:T(8,128)} custom-call(bf16[160,512]{1,0:T(8,128)(2,1)} %bitcast.5, s32[8,160]{1,0:T(8,128)} %bitcast.8, f32[9,512]{1,0:T(8,128)} %taps_in.1, f32[1,512]{1,0:T(1,128)} %bitcast.9, bf16[128,1536]{1,0:T(8,128)(2,1)} %qkv_shard.1, bf16[128,512]{1,0:T(8,128)(2,1)} %out_shard.1, bf16[10,16,512]{2,1,0:T(8,128)(2,1)} %bitcast.6), custom_call_target="tpu_custom_call" | custom-call | tf_op jit(solution)/shard_map/pallas_call | solution.py:474
  60.6 1.3 %copy.9 = f32[2048]{0:T(1024)} copy(f32[2048]{0:T(1024)} %bitcast.7) | data formatting | bytes 16384

commit v4 on v3

--- a/solution.py
+++ b/solution.py
@@ -74,11 +74,13 @@
 
 
 def place_of(group):
-    return (16 * group) // GROUPS
+    lane = group % 5
+    return (3 * lane + (group // 5) * (1 + lane // 2 - lane // 4) + 6) % 16
 
 
 def group_of(zed):
-    group = jnp.minimum((GROUPS * zed + 15) // 16, GROUPS - 1)
+    place = (zed + 10) % 16
+    group = jnp.minimum(place // 3, 4) + jnp.where(place % 3 == 0, 0, 5)
     return group, place_of(group) == zed
 
 
@@ -258,10 +260,11 @@
     def _():
         down.start()
 
-    def exchange(source, target, sems, first, count):
+    def exchange(source, target, sems, first):
         copies = []
-        for k in range(count):
-            theirs = first + (k + zed) % count
+        farthest = ((zed + 18) % 16) // 3
+        for k in (0, 1, 4, 2, 3):
+            theirs = first + (farthest + k) % 5
             to = place_of(theirs)
             copy = remote(
                 source.at[theirs], target.at[zed], sems.at[0, theirs], sems.at[1, zed], at_z(to)
@@ -295,7 +298,11 @@
         for copy in weight_copies:
             copy.start()
 
-    cot_copies = exchange(cotangent, cot_in, cot_sems, 0, GROUPS)
+    cot_copies = [
+        pair
+        for first in (0, 5)
+        for pair in exchange(cotangent, cot_in, cot_sems, first)
+    ]
     local_all = nearby[...].T - (blk * BAND - EDGE)
 
     @pl.when(blk > 0)
@@ -316,7 +323,7 @@
             hidden, gain[...]
         ).reshape(half_groups, GROUP, 512)
         normed_copies += exchange(
-            normed_out, normed_in, normed_sems, half * half_groups, half_groups
+            normed_out, normed_in, normed_sems, half * half_groups
         )
 
     @pl.when(active)
@@ -444,6 +451,17 @@
         for copy, other in threes:
             pl.when(other)(copy.wait_send)
 
+    for copy, other in cot_copies + normed_copies:
+        pl.when(other)(copy.wait_send)
+
+    @pl.when(blk > 0)
+    def _():
+        up.wait_send()
+
+    @pl.when(blk < 7)
+    def _():
+        down.wait_send()
+
     total = z_sum[zed]
     for g in range(GROUPS):
         come = place_of(g)
@@ -454,17 +472,6 @@
     for g in range(GROUPS):
         total += z_in[place_of(g)].astype(F32)
     out[...] = total
-
-    for copy, other in cot_copies + normed_copies:
-        pl.when(other)(copy.wait_send)
-
-    @pl.when(blk > 0)
-    def _():
-        up.wait_send()
-
-    @pl.when(blk < 7)
-    def _():
-        down.wait_send()
 
 
 def per_device(features, neighbours, conv_taps, norm_gain, qkv_weight, out_weight, cotangent):

time: 62.4 us -> 61.7 us (0.989)
  no operation moved by 1% of the time
where the time goes in v4:
time: 61.7 us; the launch traced here: 61.6 us
  Pallas kernels  60.3 us (98%)
  local copies, waits for them, and re-layouts  1.3 us (2%)
    pallas_call x1, Pallas kernels, per_device(): pl.pallas_call(kernel, out_shape=jax.ShapeDtypeStruct(TILE, F32), in_spec...  60.3 us
    unnamed x1, local copies, waits for them, and re-layouts  1.3 us

profile of v4, /device:TPU:1, one launch (start us, length us, event | category | flops | bytes accessed | tf_op | source)
XLA Modules:
  0.0 61.6 jit_solution(10723582900697168158)
XLA Ops:
  0.0 60.3 %shard_map.73 = f32[16,128]{1,0:T(8,128)} custom-call(bf16[160,512]{1,0:T(8,128)(2,1)} %bitcast.5, s32[8,160]{1,0:T(8,128)} %bitcast.8, f32[9,512]{1,0:T(8,128)} %taps_in.1, f32[1,512]{1,0:T(1,128)} %bitcast.9, bf16[128,1536]{1,0:T(8,128)(2,1)} %qkv_shard.1, bf16[128,512]{1,0:T(8,128)(2,1)} %out_shard.1, bf16[10,16,512]{2,1,0:T(8,128)(2,1)} %bitcast.6), custom_call_target="tpu_custom_call" | custom-call | tf_op jit(solution)/shard_map/pallas_call | solution.py:481
  60.3 1.3 %copy.9 = f32[2048]{0:T(1024)} copy(f32[2048]{0:T(1024)} %bitcast.7) | data formatting | bytes 16384

commit v5 on v4

--- a/solution.py
+++ b/solution.py
@@ -212,40 +212,18 @@
         for copy in held:
             copy.start()
 
-    near[2 * EDGE + BAND :] = jnp.zeros((NEAR - 2 * EDGE - BAND, 512), BF16)
-    z_in[...] = jnp.zeros_like(z_in)
-
-    @pl.when(blk == 0)
-    def _():
-        near[0:EDGE] = jnp.zeros((EDGE, 512), BF16)
-
-    @pl.when(blk == 7)
-    def _():
-        near[EDGE + BAND : 2 * EDGE + BAND] = jnp.zeros((EDGE, 512), BF16)
-
-    @pl.when(active)
-    def _():
-        bias[...] = causal_bias()
-
-    @pl.when(jnp.logical_not(active))
-    def _():
-        z_sum[...] = jnp.zeros_like(z_sum)
-
-    for copy in owned:
-        copy.wait()
-
     extra = jnp.where((blk == 3) | (blk == 4), 1, 0)
     pl.semaphore_wait(barrier, len(partners) + extra)
 
     up = remote(
-        near.at[EDGE : 2 * EDGE],
+        features.at[0:EDGE],
         near.at[EDGE + BAND : 2 * EDGE + BAND],
         halo_sems.at[0, 0],
         halo_sems.at[1, 0],
         (jnp.maximum(blk - 1, 0), zed, fsdp),
     )
     down = remote(
-        near.at[BAND : EDGE + BAND],
+        features.at[BAND - EDGE : BAND],
         near.at[0:EDGE],
         halo_sems.at[0, 1],
         halo_sems.at[1, 1],
@@ -303,6 +281,27 @@
         for first in (0, 5)
         for pair in exchange(cotangent, cot_in, cot_sems, first)
     ]
+    near[2 * EDGE + BAND :] = jnp.zeros((NEAR - 2 * EDGE - BAND, 512), BF16)
+    z_in[zed] = jnp.zeros(TILE, BF16)
+
+    @pl.when(blk == 0)
+    def _():
+        near[0:EDGE] = jnp.zeros((EDGE, 512), BF16)
+
+    @pl.when(blk == 7)
+    def _():
+        near[EDGE + BAND : 2 * EDGE + BAND] = jnp.zeros((EDGE, 512), BF16)
+
+    @pl.when(active)
+    def _():
+        bias[...] = causal_bias()
+
+    @pl.when(jnp.logical_not(active))
+    def _():
+        z_sum[...] = jnp.zeros_like(z_sum)
+
+    for copy in owned:
+        copy.wait()
     local_all = nearby[...].T - (blk * BAND - EDGE)
 
     @pl.when(blk > 0)
@@ -413,7 +412,7 @@
                 )
             for q in range(4):
                 sum_1[i, q] = piece_chunks(i, here, q, core) + core_in[i, here, q].astype(F32)
-        for i in range(4):
+        def send_second(i):
             for copy in ones[3 * i : 3 * i + 3]:
                 copy.wait_recv()
             for q in range(4):
@@ -428,7 +427,8 @@
                 twos.append(
                     send(out_2.at[i, to], in_2.at[i, d - 1], two_sems, 3 * i + d - 1, at(to))
                 )
-        for i in range(4):
+
+        def send_third(i):
             for copy in twos[3 * i : 3 * i + 3]:
                 copy.wait_recv()
             here, at = along(i, False)
@@ -445,6 +445,15 @@
                 other = to != zed
                 pl.when(other)(copy.start)
                 threes.append((copy, other))
+
+        send_second(0)
+        send_second(1)
+        send_third(0)
+        send_second(2)
+        send_third(1)
+        send_second(3)
+        send_third(2)
+        send_third(3)
 
         for copy in weight_copies + passed + zeros + ones + twos:
             copy.wait_send()

time: 61.7 us -> 61.8 us (level)
  no operation moved by 1% of the time
where the time goes in v5:
time: 61.8 us; the launch traced here: 61.6 us
  Pallas kernels  60.3 us (98%)
  local copies, waits for them, and re-layouts  1.3 us (2%)
    pallas_call x1, Pallas kernels, per_device(): pl.pallas_call(kernel, out_shape=jax.ShapeDtypeStruct(TILE, F32), in_spec...  60.3 us
    unnamed x1, local copies, waits for them, and re-layouts  1.3 us

profile of v5, /device:TPU:1, one launch (start us, length us, event | category | flops | bytes accessed | tf_op | source)
XLA Modules:
  0.0 61.6 jit_solution(6281747103872134786)
XLA Ops:
  0.0 60.3 %shard_map.73 = f32[16,128]{1,0:T(8,128)} custom-call(bf16[160,512]{1,0:T(8,128)(2,1)} %bitcast.5, s32[8,160]{1,0:T(8,128)} %bitcast.8, f32[9,512]{1,0:T(8,128)} %taps_in.1, f32[1,512]{1,0:T(1,128)} %bitcast.9, bf16[128,1536]{1,0:T(8,128)(2,1)} %qkv_shard.1, bf16[128,512]{1,0:T(8,128)(2,1)} %out_shard.1, bf16[10,16,512]{2,1,0:T(8,128)(2,1)} %bitcast.6), custom_call_target="tpu_custom_call" | custom-call | tf_op jit(solution)/shard_map/pallas_call | solution.py:490
  60.3 1.3 %copy.9 = f32[2048]{0:T(1024)} copy(f32[2048]{0:T(1024)} %bitcast.7) | data formatting | bytes 16384
